TPU v7x, 512 devices: a whole 4x4x16 slice. The times are simulated.
512 devices in a mesh: half: 2 (over core), row: 16 (over z), col: 16 (over y, x).
Axes of the slice: x: 4, y: 4, z: 16, core: 2. Of those that a mesh axis runs over, the one named last changes fastest.
Arguments:
- child_front: float32 [2, 8192, 8192], P('half', 'row', 'col'), as said below
- child_map: int32 [2, 48], P('half'), may hold values from 0 to 63, as said below
- root_front: float32 [8192, 16, 2, 256], P('row', 'col', 'half'), as said below
Outputs:
- child_panel: float32 [2, 512, 8192], P('half', None, 'col')
- root_panel: float32 [512, 16, 2, 256], P(None, 'col', 'half')
- root_update: float32 [8192, 16, 2, 256], P('row', 'col', 'half')
Inputs may be any that keep to these rules, and one draw needn't show every extreme that they name: `child_map`: for child h, the update blocks of row part k (the 3 blocks after that part's first block) map in increasing order to distinct blocks among the root's blocks k * 4 to (k + 1) * 4 - 1. `child_front`: each child's front is symmetric and positive definite. `root_front`: the root front is symmetric and positive definite.
All inputs are finite; a program needn't handle non-finite values.
Results may differ from a plain program's by a relative error of at most 0.0001.
Values sent between devices are 32-bit elements; how exact they have to be, the bound alone decides.
A program may use at most 64 MiB of HBM per device.

v0:
```python
import jax
import jax.numpy as jnp
from jax import lax
from jax.sharding import PartitionSpec as P

BLK = 128
PB = 32


def spread_2(value, axis, source):
    kept = jnp.where(lax.axis_index(axis) == source, value, 0).astype(value.dtype)
    return lax.psum(kept, axis)


def lower_solve(factor, right):
    return lax.linalg.triangular_solve(factor, right, left_side=True, lower=True)


def transposed_product(left, right):
    return lax.dot_general(
        left,
        right,
        (((0,), (0,)), ((), ())),
        precision=lax.Precision.HIGHEST,
        preferred_element_type=jnp.float32,
    )


def selector(child_row_map, part_index, child_tiles, root_tiles):
    per_part = child_tiles - 1
    targets = (
        lax.dynamic_slice_in_dim(child_row_map, part_index * per_part, per_part)
        - part_index * root_tiles
    )
    one_hot = (jnp.arange(root_tiles, dtype=jnp.int32)[:, None] == targets[None, :]).astype(
        jnp.float32
    )
    return jnp.concatenate([jnp.zeros((root_tiles, 1), jnp.float32), one_hot], axis=1)


def body(child_front, child_map, root_front):
    tile_rows = BLK
    pivot_count = PB
    child_block = child_front[0]
    part_rows = child_block.shape[0]
    row_part = lax.axis_index("row")
    col_part = lax.axis_index("col")
    strips = lax.all_gather(child_block[:pivot_count, :], "row", axis=0, tiled=True)
    pieces = lax.all_gather(
        child_block[None, :pivot_count, :pivot_count], ("row", "col"), axis=0, tiled=True
    )
    parts_count = lax.axis_size("row")
    corner = pieces.reshape(parts_count, parts_count, pivot_count, pivot_count).transpose(
        0, 2, 1, 3
    )
    corner = corner.reshape(parts_count * pivot_count, parts_count * pivot_count)
    factor = jnp.linalg.cholesky(corner)
    child_panel = lower_solve(factor, strips)
    columns = lax.all_gather(child_block[:, :pivot_count], "col", axis=1, tiled=True)
    panel_rows = lower_solve(factor, columns.T)
    update = child_block - transposed_product(panel_rows, child_panel)
    root_rows = root_front.shape[0]
    child_tiles = part_rows // tile_rows
    root_tiles = root_rows // tile_rows
    own_map = child_map[0]
    row_select = selector(own_map, row_part, child_tiles, root_tiles)
    col_select = selector(own_map, col_part, child_tiles, root_tiles)
    blocks = update.reshape(child_tiles, tile_rows, child_tiles, tile_rows)
    spread = jnp.einsum("ap,piqj->aiqj", row_select, blocks, precision=lax.Precision.HIGHEST)
    spread = jnp.einsum("aiqj,bq->aibj", spread, col_select, precision=lax.Precision.HIGHEST)
    additions = spread.reshape(root_rows, 2, root_rows // 2)
    joined = lax.psum_scatter(additions, "half", scatter_dimension=1, tiled=True)
    assembled = root_front[:, 0, 0, :] + joined[:, 0, :]
    root_strips = lax.all_gather(assembled[:pivot_count, :], "row", axis=0, tiled=True)
    pivots = spread_2(root_strips[:, :pivot_count], "half", 0)
    root_corner = lax.all_gather(pivots, "col", axis=1, tiled=True)
    root_factor = jnp.linalg.cholesky(root_corner)
    root_panel = lower_solve(root_factor, root_strips)
    mirrored = spread_2(root_panel, "col", row_part)
    both_halves = lax.all_gather(mirrored[:, None, :], "half", axis=1, tiled=True)
    panel_side = both_halves.reshape(both_halves.shape[0], root_rows)
    root_update = assembled - transposed_product(panel_side, root_panel)
    return (child_panel[None], root_panel[:, None, None, :], root_update[:, None, None, :])


def solution(mesh):
    return jax.shard_map(
        body,
        mesh=mesh,
        in_specs=(P("half", "row", "col"), P("half", None), P("row", "col", "half", None)),
        out_specs=(
            P("half", None, "col"),
            P(None, "col", "half", None),
            P("row", "col", "half", None),
        ),
        check_vma=False,
    )
```

profile of v0, /device:TPU:1, one launch (start us, length us, event | category | flops | bytes accessed | tf_op | source)
XLA Modules:
  0.0 844.2 jit_solution(4435899986150828886)
XLA Ops:
  12.8 208.7 %all-gather.14.cloned.1.call-done = f32[8192,32]{1,0:T(8,128)} async-done(((f32[32,32]{1,0:T(8,128)}), f32[8192,32]{1,0:T(8,128)}) %all-gather.14.cloned.1.call-update) | async-done | bytes 1048592 | tf_op jit(solution)/shard_map/all_gather | solution.py:49
  232.2 11.7 %cholesky.286 = f32[128,128]{1,0:T(8,128)S(1)} custom-call(f32[128,128]{1,0:T(8,128)S(1)} %cholesky.426), custom_call_target="Cholesky" | custom-call | tf_op jit(solution)/shard_map/jit(cholesky)/cholesky | solution.py:57
  244.0 9.8 %custom-call.31 = f32[1,128,128]{1,2,0:T(8,128)S(1)} custom-call(f32[1,128,128]{2,1,0:T(8,128)S(1)} %get-tuple-element.79), custom_call_target="InvertDiagBlocksLowerTriangular" | custom-call | tf_op jit(solution)/shard_map/jit(cholesky)/cholesky | solution.py:57
  256.4 11.7 %cholesky.305 = f32[128,128]{1,0:T(8,128)S(1)} custom-call(f32[128,128]{1,0:T(8,128)S(1)} %cholesky.430), custom_call_target="Cholesky" | custom-call | tf_op jit(solution)/shard_map/jit(cholesky)/cholesky | solution.py:57
  268.2 10.0 %custom-call.32 = f32[1,128,128]{1,2,0:T(8,128)S(1)} custom-call(f32[1,128,128]{2,1,0:T(8,128)S(1)} %get-tuple-element.76), custom_call_target="InvertDiagBlocksLowerTriangular" | custom-call | tf_op jit(solution)/shard_map/jit(cholesky)/cholesky | solution.py:57
  279.7 11.7 %cholesky.326 = f32[128,128]{1,0:T(8,128)S(1)} custom-call(f32[128,128]{1,0:T(8,128)S(1)} %cholesky.435), custom_call_target="Cholesky" | custom-call | tf_op jit(solution)/shard_map/jit(cholesky)/cholesky | solution.py:57
  292.2 9.8 %custom-call.33 = f32[1,128,128]{1,2,0:T(8,128)S(1)} custom-call(f32[1,128,128]{2,1,0:T(8,128)S(1)} %get-tuple-element.73), custom_call_target="InvertDiagBlocksLowerTriangular" | custom-call | tf_op jit(solution)/shard_map/jit(cholesky)/cholesky | solution.py:57
  303.5 11.7 %cholesky.343 = f32[128,128]{1,0:T(8,128)S(1)} custom-call(f32[128,128]{1,0:T(8,128)S(1)} %convolution_subtract_fusion.16), custom_call_target="Cholesky" | custom-call | tf_op jit(solution)/shard_map/jit(cholesky)/cholesky | solution.py:57
  319.6 8.5 %while.6 = (s32[]{:T(128)}, f32[512,512]{1,0:T(8,128)S(1)}, s32[4,2]{0,1:T(2,128)S(1)}, f32[4,128,128]{2,1,0:T(8,128)S(1)}, s32[]{:T(128)}) while((s32[]{:T(128)}, f32[512,512]{1,0:T(8,128)S(1)}, s32[4,2]{0,1:T(2,128)S(1)}, f32[4,128,128]{2,1,0:T(8,128)S(1)}, s32[]{:T(128)}) %tuple.64), condition=%wide.while_cond, body=%wide.while_body.sunk | while | flops 2 | bytes 131181 | solution.py:16
  328.1 39.3 %custom-call.34 = f32[4,128,128]{1,2,0:T(8,128)S(1)} custom-call(f32[4,128,128]{2,1,0:T(8,128)S(1)} %get-tuple-element.27), custom_call_target="InvertDiagBlocksLowerTriangular" | custom-call | tf_op jit(solution)/shard_map/triangular_solve/custom-call.3 | solution.py:16
  392.0 23.3 %reduce-scatter.2.cloned.1.call-done = f32[512,1,256]{2,0,1:T(8,128)} async-done(((f32[512,2,256]{2,0,1:T(8,128)}), f32[512,1,256]{2,0,1:T(8,128)}) %reduce-scatter.2.cloned.1.call-update) | async-done | bytes 524304 | tf_op jit(solution)/shard_map/reduce_scatter | solution.py:72
  417.2 25.4 %all_gather.21 = f32[512,256]{1,0:T(8,128)S(1)} all-gather(f32[32,256]{1,0:T(8,128)S(1)} %slice.211), channel_id=1, replica_groups=mesh['half'=2,'row'=16,'col'=16] {'row'}, dimensions={0}, use_global_device_ids=true | all-gather | bytes 557056 | tf_op jit(solution)/shard_map/all_gather | solution.py:74
  443.4 44.3 %all-reduce.6.cloned.1.call-done = f32[512,32]{0,1:T(8,128)} async-done(((f32[512,32]{0,1:T(8,128)}), f32[512,32]{0,1:T(8,128)}) %all-reduce.6.cloned.1.call-update) | async-done | bytes 65552 | tf_op jit(solution)/shard_map/psum | solution.py:12
  487.9 59.6 %all-gather.10.cloned.1.call-done = f32[512,512]{0,1:T(8,128)} async-done(((f32[512,32]{0,1:T(8,128)}), f32[512,512]{0,1:T(8,128)}) %all-gather.10.cloned.1.call-update) | async-done | bytes 1048592 | tf_op jit(solution)/shard_map/all_gather | solution.py:76
  550.5 11.7 %cholesky.358 = f32[128,128]{1,0:T(8,128)S(1)} custom-call(f32[128,128]{1,0:T(8,128)S(1)} %cholesky.439), custom_call_target="Cholesky" | custom-call | tf_op jit(solution)/shard_map/jit(cholesky)/cholesky | solution.py:77
  562.4 9.8 %custom-call.36 = f32[1,128,128]{1,2,0:T(8,128)S(1)} custom-call(f32[1,128,128]{2,1,0:T(8,128)S(1)} %get-tuple-element.69), custom_call_target="InvertDiagBlocksLowerTriangular" | custom-call | tf_op jit(solution)/shard_map/jit(cholesky)/cholesky | solution.py:77
  573.6 11.7 %cholesky.377 = f32[128,128]{1,0:T(8,128)S(1)} custom-call(f32[128,128]{1,0:T(8,128)S(1)} %cholesky.443), custom_call_target="Cholesky" | custom-call | tf_op jit(solution)/shard_map/jit(cholesky)/cholesky | solution.py:77
  586.7 10.0 %custom-call.37 = f32[1,128,128]{1,2,0:T(8,128)S(1)} custom-call(f32[1,128,128]{2,1,0:T(8,128)S(1)} %get-tuple-element.66), custom_call_target="InvertDiagBlocksLowerTriangular" | custom-call | tf_op jit(solution)/shard_map/jit(cholesky)/cholesky | solution.py:77
  598.8 13.2 %cholesky.398 = f32[128,128]{1,0:T(8,128)} custom-call(f32[128,128]{1,0:T(8,128)} %cholesky.448), custom_call_target="Cholesky" | custom-call | tf_op jit(solution)/shard_map/jit(cholesky)/cholesky | solution.py:77
  614.2 11.3 %custom-call.38 = f32[1,128,128]{1,2,0:T(8,128)} custom-call(f32[1,128,128]{2,1,0:T(8,128)} %get-tuple-element.63), custom_call_target="InvertDiagBlocksLowerTriangular" | custom-call | tf_op jit(solution)/shard_map/jit(cholesky)/cholesky | solution.py:77
  626.9 11.7 %cholesky.415 = f32[128,128]{1,0:T(8,128)S(1)} custom-call(f32[128,128]{1,0:T(8,128)S(1)} %convolution_subtract_fusion.15), custom_call_target="Cholesky" | custom-call | tf_op jit(solution)/shard_map/jit(cholesky)/cholesky | solution.py:77
  650.2 39.3 %custom-call.26 = f32[4,128,128]{1,2,0:T(8,128)S(1)} custom-call(f32[4,128,128]{2,1,0:T(8,128)S(1)} %get-tuple-element.20), custom_call_target="InvertDiagBlocksLowerTriangular" | custom-call | tf_op jit(solution)/shard_map/triangular_solve | solution.py:16
  693.7 115.5 %all-reduce.8.cloned.1.call-done = f32[512,1,256]{2,0,1:T(8,128)} async-done(((f32[512,1,256]{2,0,1:T(8,128)}), f32[512,1,256]{2,0,1:T(8,128)}) %all-reduce.8.cloned.1.call-update) | async-done | bytes 524304 | tf_op jit(solution)/shard_map/psum | solution.py:12
  812.5 20.5 %all-gather.12.cloned.1.call-done = f32[512,2,256]{2,0,1:T(8,128)} async-done(((f32[512,1,256]{2,0,1:T(8,128)}), f32[512,2,256]{2,0,1:T(8,128)}) %all-gather.12.cloned.1.call-update) | async-done | bytes 1048592 | tf_op jit(solution)/shard_map/all_gather | solution.py:80
  (154 shorter events, 100.0 us)
Async XLA Ops:
  7.2 214.4 %all-gather.14.cloned.1.call-start = ((), (), s32[]{:S(2)}) async-start(), calls=%async_computation.7 | async-start | bytes 4210688 | tf_op jit(solution)/shard_map/all_gather | solution.py:49
  8.6 358.9 %all-gather.8.cloned.1.call-start = ((), (), s32[]{:S(2)}) async-start(), calls=%async_computation.1 | async-start | bytes 1114112 | tf_op jit(solution)/shard_map/all_gather | solution.py:59
  10.3 365.5 %all-gather.16.cloned.1.call-start = ((), (), s32[]{:S(2)}) async-start(), calls=%async_computation.8 | async-start | bytes 1114112 | tf_op jit(solution)/shard_map/all_gather | solution.py:48
  11.9 403.3 %reduce-scatter.2.cloned.1.call-start = ((), (), s32[]{:S(2)}) async-start(), calls=%async_computation.2 | async-start | bytes 1572864 | tf_op jit(solution)/shard_map/reduce_scatter | solution.py:72
  231.2 1.0 copy-start
  372.4 0.7 copy-start.3
  375.8 7.7 copy-start.4
  375.8 7.7 copy-start.9
  382.9 0.7 copy-start.5
  388.7 26.5 %copy-start.7 = (f32[512,1,1,256]{3,2,1,0:T(1,128)S(1)}, f32[512,1,1,256]{3,2,1,0:T(1,128)}, u32[]{:S(2)}) copy-start(f32[512,1,1,256]{3,2,1,0:T(1,128)} %param.8) | copy-start | bytes 1572868
  391.9 95.8 %all-reduce.6.cloned.1.call-start = ((), (), s32[]{:S(2)}) async-start(), calls=%async_computation.3 | async-start | bytes 131072 | tf_op jit(solution)/shard_map/psum | solution.py:12
  416.4 0.8 copy-start.1
  443.3 104.2 %all-gather.10.cloned.1.call-start = ((), (), s32[]{:S(2)}) async-start(), calls=%async_computation.4 | async-start | bytes 1114112 | tf_op jit(solution)/shard_map/all_gather | solution.py:76
  487.7 321.4 %all-reduce.8.cloned.1.call-start = ((), (), s32[]{:S(2)}) async-start(), calls=%async_computation.5 | async-start | bytes 1048576 | tf_op jit(solution)/shard_map/psum | solution.py:12
  572.9 0.7 copy-start.6
  689.6 1.5 copy-start.8
  691.5 143.1 %copy-start.2 = (f32[512,256]{1,0:T(8,128)S(1)}, f32[512,256]{1,0:T(8,128)}, u32[]{:S(2)}) copy-start(f32[512,256]{1,0:T(8,128)} %copy-done.1) | copy-start | bytes 1572868
  693.6 139.4 %all-gather.12.cloned.1.call-start = ((), (), s32[]{:S(2)}) async-start(), calls=%async_computation.6 | async-start | bytes 1572864 | tf_op jit(solution)/shard_map/all_gather | solution.py:80
Sparse Core Ops, SparseCore 0:
  13.1 208.4 all-gather.13
  225.1 59.4 all-gather.7
  287.2 63.2 all-gather.15
  392.0 23.1 reduce-scatter.1
  443.5 44.1 all-reduce.5
  491.0 56.4 all-gather.9
  693.7 115.3 all-reduce.7
  811.2 21.7 all-gather.11
where the time goes:
time: 855 us; the launch traced here: 844 us
  waiting for transfers between devices  472 us (55%)
  other arithmetic  248 us (29%)
  local copies, waits for them, and re-layouts  43.7 us (5%)
  matrix products  33.6 us (4%)
  blocking collectives  25.4 us (3%)
  between operations  20.3 us (2%)
    all_gather x1, waiting for transfers between devices, body(): lax.all_gather(child_block[None, :pivot_count, :pivot_count], ('row', 'co...  209 us
    psum x2, waiting for transfers between devices, spread_2(): return lax.psum(kept, axis)  160 us
    another operation x15, other arithmetic, body(): root_factor = jnp.linalg.cholesky(root_corner)  83.6 us
    another operation x5, other arithmetic, lower_solve(): lax.linalg.triangular_solve(factor, right, left_side=True, lower=True)  79.1 us
    another operation x14, other arithmetic, body(): factor = jnp.linalg.cholesky(corner)  78.6 us
    all_gather x1, waiting for transfers between devices, body(): root_corner = lax.all_gather(pivots, 'col', axis=1, tiled=True)  59.6 us
    all_gather x1, blocking collectives, body(): lax.all_gather(assembled[:pivot_count, :], 'row', axis=0, tiled=True)  25.4 us
    reduce_scatter x1, waiting for transfers between devices, body(): lax.psum_scatter(additions, 'half', scatter_dimension=1, tiled=True)  23.3 us
  transfers between devices with their start and end apart: 8, of which 6 were waited for; matrix products, arithmetic and copies ran while one was open for 19% of the time, Pallas kernels for 0%

commit v1 on v0

--- a/solution.py
+++ b/solution.py
@@ -73,7 +73,9 @@
     assembled = root_front[:, 0, 0, :] + joined[:, 0, :]
     root_strips = lax.all_gather(assembled[:pivot_count, :], "row", axis=0, tiled=True)
     pivots = spread_2(root_strips[:, :pivot_count], "half", 0)
-    root_corner = lax.all_gather(pivots, "col", axis=1, tiled=True)
+    root_corner = jnp.concatenate(
+        lax.all_to_all(jnp.stack([pivots] * lax.axis_size("col")), "col", 0, 0), axis=1
+    )
     root_factor = jnp.linalg.cholesky(root_corner)
     root_panel = lower_solve(root_factor, root_strips)
     mirrored = spread_2(root_panel, "col", row_part)

time: 855 us -> 813 us (0.951)
  waiting for transfers between devices: 472 us -> 428 us
    all_gather x1 -> x0, waiting for transfers between devices: 59.6 us -> none  [body(): root_corner = lax.all_gather(pivots, 'col', axis=1, tiled=True)]
    all_to_all x0 -> x1, waiting for transfers between devices: none -> 16.3 us  [body(): lax.all_to_all(jnp.stack([pivots] * lax.axis_size('col')), 'col', 0, 0)]
  transfers between devices with their start and end apart: 8 -> 8, of which waited for: 6 -> 6; matrix products, arithmetic and copies ran while one was open for 19% -> 20% of each run, Pallas kernels for 0% -> 0%
where the time goes in v1:
time: 813 us; the launch traced here: 802 us
  waiting for transfers between devices  428 us (53%)
  other arithmetic  243 us (30%)
  local copies, waits for them, and re-layouts  43.8 us (5%)
  matrix products  35.5 us (4%)
  blocking collectives  25.4 us (3%)
  between operations  20.3 us (2%)
    all_gather x1, waiting for transfers between devices, body(): lax.all_gather(child_block[None, :pivot_count, :pivot_count], ('row', 'co...  209 us
    psum x2, waiting for transfers between devices, spread_2(): return lax.psum(kept, axis)  159 us
    another operation x5, other arithmetic, lower_solve(): lax.linalg.triangular_solve(factor, right, left_side=True, lower=True)  79.5 us
    another operation x15, other arithmetic, body(): root_factor = jnp.linalg.cholesky(root_corner)  79.2 us
    another operation x14, other arithmetic, body(): factor = jnp.linalg.cholesky(corner)  78.6 us
    all_gather x1, blocking collectives, body(): lax.all_gather(assembled[:pivot_count, :], 'row', axis=0, tiled=True)  25.4 us
    reduce_scatter x1, waiting for transfers between devices, body(): lax.psum_scatter(additions, 'half', scatter_dimension=1, tiled=True)  23.3 us
    all_gather x1, waiting for transfers between devices, body(): lax.all_gather(mirrored[:, None, :], 'half', axis=1, tiled=True)  20.7 us
  transfers between devices with their start and end apart: 8, of which 6 were waited for; matrix products, arithmetic and copies ran while one was open for 20% of the time, Pallas kernels for 0%

profile of v1, /device:TPU:1, one launch (start us, length us, event | category | flops | bytes accessed | tf_op | source)
XLA Modules:
  0.0 802.4 jit_solution(15668333136225276405)
XLA Ops:
  12.8 208.7 %all-gather.11.cloned.1.call-done = f32[8192,32]{1,0:T(8,128)} async-done(((f32[32,32]{1,0:T(8,128)}), f32[8192,32]{1,0:T(8,128)}) %all-gather.11.cloned.1.call-update) | async-done | bytes 1048592 | tf_op jit(solution)/shard_map/all_gather | solution.py:49
  232.2 11.7 %cholesky.286 = f32[128,128]{1,0:T(8,128)S(1)} custom-call(f32[128,128]{1,0:T(8,128)S(1)} %cholesky.426), custom_call_target="Cholesky" | custom-call | tf_op jit(solution)/shard_map/jit(cholesky)/cholesky | solution.py:57
  244.0 9.8 %custom-call.31 = f32[1,128,128]{1,2,0:T(8,128)S(1)} custom-call(f32[1,128,128]{2,1,0:T(8,128)S(1)} %get-tuple-element.79), custom_call_target="InvertDiagBlocksLowerTriangular" | custom-call | tf_op jit(solution)/shard_map/jit(cholesky)/cholesky | solution.py:57
  256.4 11.7 %cholesky.305 = f32[128,128]{1,0:T(8,128)S(1)} custom-call(f32[128,128]{1,0:T(8,128)S(1)} %cholesky.430), custom_call_target="Cholesky" | custom-call | tf_op jit(solution)/shard_map/jit(cholesky)/cholesky | solution.py:57
  268.2 10.0 %custom-call.32 = f32[1,128,128]{1,2,0:T(8,128)S(1)} custom-call(f32[1,128,128]{2,1,0:T(8,128)S(1)} %get-tuple-element.76), custom_call_target="InvertDiagBlocksLowerTriangular" | custom-call | tf_op jit(solution)/shard_map/jit(cholesky)/cholesky | solution.py:57
  279.7 11.7 %cholesky.326 = f32[128,128]{1,0:T(8,128)S(1)} custom-call(f32[128,128]{1,0:T(8,128)S(1)} %cholesky.435), custom_call_target="Cholesky" | custom-call | tf_op jit(solution)/shard_map/jit(cholesky)/cholesky | solution.py:57
  292.2 9.8 %custom-call.33 = f32[1,128,128]{1,2,0:T(8,128)S(1)} custom-call(f32[1,128,128]{2,1,0:T(8,128)S(1)} %get-tuple-element.73), custom_call_target="InvertDiagBlocksLowerTriangular" | custom-call | tf_op jit(solution)/shard_map/jit(cholesky)/cholesky | solution.py:57
  303.5 11.7 %cholesky.343 = f32[128,128]{1,0:T(8,128)S(1)} custom-call(f32[128,128]{1,0:T(8,128)S(1)} %convolution_subtract_fusion.16), custom_call_target="Cholesky" | custom-call | tf_op jit(solution)/shard_map/jit(cholesky)/cholesky | solution.py:57
  319.2 8.5 %while.6 = (s32[]{:T(128)}, f32[512,512]{1,0:T(8,128)S(1)}, s32[4,2]{0,1:T(2,128)S(1)}, f32[4,128,128]{2,1,0:T(8,128)S(1)}, s32[]{:T(128)}) while((s32[]{:T(128)}, f32[512,512]{1,0:T(8,128)S(1)}, s32[4,2]{0,1:T(2,128)S(1)}, f32[4,128,128]{2,1,0:T(8,128)S(1)}, s32[]{:T(128)}) %tuple.64), condition=%wide.while_cond, body=%wide.while_body.sunk | while | flops 2 | bytes 131181 | solution.py:16
  327.7 39.7 %custom-call.34 = f32[4,128,128]{1,2,0:T(8,128)S(1)} custom-call(f32[4,128,128]{2,1,0:T(8,128)S(1)} %get-tuple-element.27), custom_call_target="InvertDiagBlocksLowerTriangular" | custom-call | tf_op jit(solution)/shard_map/triangular_solve/custom-call.3 | solution.py:16
  392.0 23.3 %reduce-scatter.2.cloned.1.call-done = f32[512,1,256]{2,0,1:T(8,128)} async-done(((f32[512,2,256]{2,0,1:T(8,128)}), f32[512,1,256]{2,0,1:T(8,128)}) %reduce-scatter.2.cloned.1.call-update) | async-done | bytes 524304 | tf_op jit(solution)/shard_map/reduce_scatter | solution.py:72
  417.2 25.4 %all_gather.18 = f32[512,256]{1,0:T(8,128)S(1)} all-gather(f32[32,256]{1,0:T(8,128)S(1)} %slice.211), channel_id=1, replica_groups=mesh['half'=2,'row'=16,'col'=16] {'row'}, dimensions={0}, use_global_device_ids=true | all-gather | bytes 557056 | tf_op jit(solution)/shard_map/all_gather | solution.py:74
  443.3 44.9 %all-reduce.6.cloned.1.call-done = f32[512,32]{1,0:T(8,128)} async-done(((f32[512,32]{1,0:T(8,128)}), f32[512,32]{1,0:T(8,128)}) %all-reduce.6.cloned.1.call-update) | async-done | bytes 65552 | tf_op jit(solution)/shard_map/psum | solution.py:12
  496.1 16.3 %all-to-all-done = f32[16,512,32]{1,2,0:T(8,128)S(1)} async-done(((f32[16,512,32]{1,2,0:T(8,128)}), f32[16,512,32]{1,2,0:T(8,128)S(1)}, u32[]{:S(2)}, u32[]{:S(2)}) %all-to-all-start) | async-done | bytes 1048608 | tf_op jit(solution)/shard_map/all_to_all | solution.py:77
  514.0 11.7 %cholesky.358 = f32[128,128]{1,0:T(8,128)S(1)} custom-call(f32[128,128]{1,0:T(8,128)S(1)} %cholesky.439), custom_call_target="Cholesky" | custom-call | tf_op jit(solution)/shard_map/jit(cholesky)/cholesky | solution.py:79
  525.9 9.8 %custom-call.36 = f32[1,128,128]{1,2,0:T(8,128)S(1)} custom-call(f32[1,128,128]{2,1,0:T(8,128)S(1)} %get-tuple-element.69), custom_call_target="InvertDiagBlocksLowerTriangular" | custom-call | tf_op jit(solution)/shard_map/jit(cholesky)/cholesky | solution.py:79
  538.2 11.7 %cholesky.377 = f32[128,128]{1,0:T(8,128)S(1)} custom-call(f32[128,128]{1,0:T(8,128)S(1)} %cholesky.443), custom_call_target="Cholesky" | custom-call | tf_op jit(solution)/shard_map/jit(cholesky)/cholesky | solution.py:79
  551.3 10.0 %custom-call.37 = f32[1,128,128]{1,2,0:T(8,128)S(1)} custom-call(f32[1,128,128]{2,1,0:T(8,128)S(1)} %get-tuple-element.66), custom_call_target="InvertDiagBlocksLowerTriangular" | custom-call | tf_op jit(solution)/shard_map/jit(cholesky)/cholesky | solution.py:79
  562.9 11.7 %cholesky.398 = f32[128,128]{1,0:T(8,128)S(1)} custom-call(f32[128,128]{1,0:T(8,128)S(1)} %cholesky.448), custom_call_target="Cholesky" | custom-call | tf_op jit(solution)/shard_map/jit(cholesky)/cholesky | solution.py:79
  575.3 9.8 %custom-call.38 = f32[1,128,128]{1,2,0:T(8,128)S(1)} custom-call(f32[1,128,128]{2,1,0:T(8,128)S(1)} %get-tuple-element.63), custom_call_target="InvertDiagBlocksLowerTriangular" | custom-call | tf_op jit(solution)/shard_map/jit(cholesky)/cholesky | solution.py:79
  586.5 11.7 %cholesky.415 = f32[128,128]{1,0:T(8,128)S(1)} custom-call(f32[128,128]{1,0:T(8,128)S(1)} %convolution_subtract_fusion.15), custom_call_target="Cholesky" | custom-call | tf_op jit(solution)/shard_map/jit(cholesky)/cholesky | solution.py:79
  609.9 39.3 %custom-call.26 = f32[4,128,128]{1,2,0:T(8,128)S(1)} custom-call(f32[4,128,128]{2,1,0:T(8,128)S(1)} %get-tuple-element.20), custom_call_target="InvertDiagBlocksLowerTriangular" | custom-call | tf_op jit(solution)/shard_map/triangular_solve | solution.py:16
  653.3 113.8 %all-reduce.8.cloned.1.call-done = f32[512,1,256]{2,0,1:T(8,128)} async-done(((f32[512,1,256]{2,0,1:T(8,128)}), f32[512,1,256]{2,0,1:T(8,128)}) %all-reduce.8.cloned.1.call-update) | async-done | bytes 524304 | tf_op jit(solution)/shard_map/psum | solution.py:12
  770.5 20.7 %all-gather.9.cloned.1.call-done = f32[512,2,256]{2,0,1:T(8,128)} async-done(((f32[512,1,256]{2,0,1:T(8,128)}), f32[512,2,256]{2,0,1:T(8,128)}) %all-gather.9.cloned.1.call-update) | async-done | bytes 1048592 | tf_op jit(solution)/shard_map/all_gather | solution.py:82
  (153 shorter events, 104.9 us)
Async XLA Ops:
  7.2 214.4 %all-gather.11.cloned.1.call-start = ((), (), s32[]{:S(2)}) async-start(), calls=%async_computation.7 | async-start | bytes 4210688 | tf_op jit(solution)/shard_map/all_gather | solution.py:49
  8.6 358.9 %all-gather.7.cloned.1.call-start = ((), (), s32[]{:S(2)}) async-start(), calls=%async_computation.2 | async-start | bytes 1114112 | tf_op jit(solution)/shard_map/all_gather | solution.py:59
  10.3 365.5 %all-gather.13.cloned.1.call-start = ((), (), s32[]{:S(2)}) async-start(), calls=%async_computation.8 | async-start | bytes 1114112 | tf_op jit(solution)/shard_map/all_gather | solution.py:48
  11.9 403.3 %reduce-scatter.2.cloned.1.call-start = ((), (), s32[]{:S(2)}) async-start(), calls=%async_computation.3 | async-start | bytes 1572864 | tf_op jit(solution)/shard_map/reduce_scatter | solution.py:72
  231.2 1.0 copy-start.1
  372.4 0.7 copy-start.4
  375.8 7.7 copy-start.5
  375.8 7.7 copy-start.9
  382.9 0.7 copy-start.6
  388.7 26.5 %copy-start.7 = (f32[512,1,1,256]{3,2,1,0:T(1,128)S(1)}, f32[512,1,1,256]{3,2,1,0:T(1,128)}, u32[]{:S(2)}) copy-start(f32[512,1,1,256]{3,2,1,0:T(1,128)} %param.8) | copy-start | bytes 1572868
  391.9 96.3 %all-reduce.6.cloned.1.call-start = ((), (), s32[]{:S(2)}) async-start(), calls=%async_computation.4 | async-start | bytes 524288 | tf_op jit(solution)/shard_map/psum | solution.py:12
  416.4 0.8 copy-start.2
  490.3 22.1 %all-to-all-start = ((f32[16,512,32]{1,2,0:T(8,128)}), f32[16,512,32]{1,2,0:T(8,128)S(1)}, u32[]{:S(2)}, u32[]{:S(2)}) async-start(f32[16,512,32]{1,2,0:T(8,128)} %stack.2), calls=%async_computation.1 | async-start | bytes 2097152 | tf_op jit(solution)/shard_map/all_to_all | solution.py:77
  496.1 271.1 %all-reduce.8.cloned.1.call-start = ((), (), s32[]{:S(2)}) async-start(), calls=%async_computation.5 | async-start | bytes 1048576 | tf_op jit(solution)/shard_map/psum | solution.py:12
  513.0 1.0 copy-start
  649.2 1.5 copy-start.8
  651.1 141.6 %copy-start.3 = (f32[512,256]{1,0:T(8,128)S(1)}, f32[512,256]{1,0:T(8,128)}, u32[]{:S(2)}) copy-start(f32[512,256]{1,0:T(8,128)} %copy-done.2) | copy-start | bytes 1572868
  653.3 137.9 %all-gather.9.cloned.1.call-start = ((), (), s32[]{:S(2)}) async-start(), calls=%async_computation.6 | async-start | bytes 1572864 | tf_op jit(solution)/shard_map/all_gather | solution.py:82
Sparse Core Ops, SparseCore 0:
  13.1 208.4 all-gather.10
  225.1 59.4 all-gather.6
  287.2 63.3 all-gather.12
  392.0 23.1 reduce-scatter.1
  443.4 44.7 all-reduce.5
  653.4 113.7 all-reduce.7
  769.4 21.7 all-gather.8
